TPU v7x, 32 devices: a whole 2x2x4 slice. The times are simulated.
32 devices in a mesh: dp: 2 (over y), seq: 16 (over z, x, core).
Axes of the slice: x: 2, y: 2, z: 4, core: 2. Of those that a mesh axis runs over, the one named last changes fastest.
Arguments:
- query_rows: bfloat16 [2, 2560, 1024], P('dp', 'seq'), may hold values from -8 to 8
- key_rows: bfloat16 [2, 2560, 128], P('dp', 'seq'), may hold values from -8 to 8
- value_rows: bfloat16 [2, 2560, 128], P('dp', 'seq'), may hold values from -6 to 6
- out_cotangent: bfloat16 [2, 2560, 1024], P('dp', 'seq'), may hold values from -6 to 6
- turn_lengths: int32 [2, 8], P('dp'), may hold values from 1 to 1280, 2560 in all within a row
- ssm_input: bfloat16 [2, 2560, 256], P('dp', 'seq'), may hold values from -6 to 6
- state_input: bfloat16 [2, 2560, 128], P('dp', 'seq'), may hold values from -0.5 to 0.5
- state_readout: bfloat16 [2, 2560, 128], P('dp', 'seq'), may hold values from -0.5 to 0.5
- log_decay: float32 [2, 4, 2560], P('dp', None, 'seq'), may hold values from -1.2 to 0, as said below
- skip_gain: float32 [4], replicated, may hold values from 0.5 to 1.5
- conv_weight: float32 [4, 256], replicated, may hold values from -3 to 3
- ssm_cotangent: bfloat16 [2, 2560, 256], P('dp', 'seq'), may hold values from -6 to 6
Outputs:
- query_grad: bfloat16 [2, 2560, 1024], P('dp', 'seq')
- key_grad: bfloat16 [2, 2560, 128], P('dp', 'seq')
- value_grad: bfloat16 [2, 2560, 128], P('dp', 'seq')
- input_grad: bfloat16 [2, 2560, 256], P('dp', 'seq')
- state_input_grad: float32 [2, 2560, 128], P('dp', 'seq')
- readout_grad: float32 [2, 2560, 128], P('dp', 'seq')
- decay_grad: float32 [2, 4, 2560], P('dp', None, 'seq')
- skip_grad: float32 [4], replicated
- conv_grad: float32 [4, 256], replicated
Inputs may be any that keep to these rules, and one draw needn't show every extreme that they name: `turn_lengths`: each transcript's 8 turn lengths sum to 2560, the longest is exactly 1280. `log_decay`: negative.
All inputs are finite; a program needn't handle non-finite values.
Results may differ from a plain program's by a relative error of at most 0.01.
Values may be sent and summed in bfloat16 or wider, within the bound.
A program may use at most 64 MiB of HBM per device.

v0:
```python
from functools import partial
import math

import jax
import jax.numpy as jnp
from jax import lax
from jax.sharding import PartitionSpec as P

KVH = 1
QPG = 8
DH = 128
SH = 4
P_SIZE = 64
N = 128
CONV = 4


NEG_FILL = -1e30


def passed_along(value, axis, by):
    length = lax.axis_size(axis)
    pairs = [(i, i + by) for i in range(length) if 0 <= i + by < length]
    return lax.ppermute(value, axis, pairs)


def prefix_2(part, axis, combine, identity):
    count = lax.axis_size(axis)
    place = lax.axis_index(axis)
    ahead = count - 1 - place
    gathered = jax.tree.map(lambda a: lax.all_gather(a, axis), part)
    state = jax.tree.map(lambda a, e: jnp.zeros_like(a) + jnp.asarray(e, a.dtype), part, identity)

    def one(turn, state):
        source = count - 1 - turn
        return combine(
            state, jax.tree.map(lambda a: lax.dynamic_index_in_dim(a, source, 0, False), gathered)
        )

    return lax.fori_loop(0, ahead, one, state)


def turn_index(turn_lengths, positions):
    bounds = jnp.cumsum(turn_lengths)
    return jnp.sum((positions[:, None] >= bounds[None, :]).astype(jnp.int32), axis=1)


def chain_combine(earlier, later):
    return (earlier[0] * later[0], later[0][:, None, None] * earlier[1] + later[1])


def attention_grads(query_rows, key_rows, value_rows, out_cotangent, turn_lengths):
    local_tok = query_rows.shape[1]
    total_rows = local_tok * lax.axis_size("seq")
    lengths = turn_lengths[0]
    scale = DH ** (-0.5)
    query = query_rows[0].reshape(local_tok, KVH, QPG, DH)
    cotangent = out_cotangent[0].reshape(local_tok, KVH, QPG, DH)
    own_pos = lax.axis_index("seq") * local_tok + jnp.arange(local_tok, dtype=jnp.int32)
    own_turn = turn_index(lengths, own_pos)
    all_keys, all_values = (
        lax.all_gather(key_rows[0], "seq", axis=0, tiled=True),
        lax.all_gather(value_rows[0], "seq", axis=0, tiled=True),
    )
    block_width = math.gcd(total_rows, 512)
    block_count = total_rows // block_width

    def block_keys(first_row):
        key_block = lax.dynamic_slice_in_dim(all_keys, first_row, block_width, 0).reshape(
            block_width, KVH, DH
        )
        value_block = lax.dynamic_slice_in_dim(all_values, first_row, block_width, 0).reshape(
            block_width, KVH, DH
        )
        key_pos = first_row + jnp.arange(block_width, dtype=jnp.int32)
        allowed = (key_pos[None, :] <= own_pos[:, None]) & (
            turn_index(lengths, key_pos)[None, :] == own_turn[:, None]
        )
        scores = (
            jnp.einsum("tgqd,sgd->gqts", query, key_block, preferred_element_type=jnp.float32)
            * scale
        )
        return (key_block, value_block, allowed, scores)

    def first_pass(block_index, running):
        row_top, row_mass, row_output = running
        key_block, value_block, allowed, scores = block_keys(block_index * block_width)
        masked = jnp.where(allowed, scores, NEG_FILL)
        new_top = jnp.maximum(row_top, jnp.max(masked, axis=-1))
        expo_terms = jnp.where(allowed, jnp.exp(masked - new_top[..., None]), 0.0)
        factor = jnp.exp(row_top - new_top)
        weighted = jnp.einsum(
            "gqts,sgd->gqtd",
            expo_terms,
            value_block.astype(jnp.float32),
            precision=lax.Precision.HIGHEST,
        )
        return (
            new_top,
            row_mass * factor + jnp.sum(expo_terms, axis=-1),
            row_output * factor[..., None] + weighted,
        )

    stat_shape = (KVH, QPG, local_tok)
    row_top, row_mass, row_output = lax.fori_loop(
        0,
        block_count,
        first_pass,
        (
            jnp.full(stat_shape, NEG_FILL, jnp.float32),
            jnp.zeros(stat_shape, jnp.float32),
            jnp.zeros(stat_shape + (DH,), jnp.float32),
        ),
    )
    row_lse = row_top + jnp.log(row_mass)
    cot_wide = jnp.transpose(cotangent, (1, 2, 0, 3)).astype(jnp.float32)
    row_delta = jnp.sum(cot_wide * row_output, axis=-1) / row_mass

    def second_pass(keep_terms, block_index, running):
        query_acc, term_rows = running
        first_row = block_index * block_width
        key_block, value_block, allowed, scores = block_keys(first_row)
        dprob = jnp.einsum(
            "tgqd,sgd->gqts", cotangent, value_block, preferred_element_type=jnp.float32
        )
        prob_f32 = jnp.where(allowed, jnp.exp(scores - row_lse[..., None]), 0.0)
        score_grad = (scale * prob_f32 * (dprob - row_delta[..., None])).astype(jnp.bfloat16)
        query_acc = query_acc + jnp.einsum(
            "gqts,sgd->tgqd", score_grad, key_block, preferred_element_type=jnp.float32
        )
        prob_bf16 = prob_f32.astype(jnp.bfloat16)
        key_term = jnp.einsum(
            "gqts,tgqd->sgd", score_grad, query, preferred_element_type=jnp.float32
        )
        value_term = jnp.einsum(
            "gqts,tgqd->sgd", prob_bf16, cotangent, preferred_element_type=jnp.float32
        )
        block_terms = jnp.concatenate(
            [key_term.reshape(block_width, KVH * DH), value_term.reshape(block_width, KVH * DH)],
            axis=1,
        )
        term_rows = lax.dynamic_update_slice_in_dim(term_rows, block_terms, first_row, 0)
        return (query_acc, term_rows)

    query_zero = jnp.zeros((local_tok, KVH, QPG, DH), jnp.float32)
    term_zero = jnp.zeros((total_rows, 2 * KVH * DH), jnp.float32)
    query_acc, term_rows = lax.fori_loop(
        0, block_count, partial(second_pass, True), (query_zero, term_zero)
    )
    summed = lax.psum_scatter(
        term_rows.astype(jnp.bfloat16), "seq", scatter_dimension=0, tiled=True
    ).astype(jnp.float32)
    key_grad = summed[:, : KVH * DH].astype(jnp.bfloat16)
    value_grad = summed[:, KVH * DH :].astype(jnp.bfloat16)
    query_grad = query_acc.reshape(local_tok, KVH * QPG * DH).astype(jnp.bfloat16)
    return (query_grad[None], key_grad[None], value_grad[None])


def ssm_grads(
    ssm_input, state_input, state_readout, log_decay, skip_gain, conv_weight, ssm_cotangent
):
    top_precision = lax.Precision.HIGHEST
    local_tok = ssm_input.shape[1]
    channels = SH * P_SIZE
    signal = ssm_input[0]
    rim_rows = passed_along(signal[local_tok - (CONV - 1) :], "seq", 1)
    padded = jnp.concatenate([rim_rows, signal], axis=0).astype(jnp.float32)
    pre_act = jnp.zeros((local_tok, channels), jnp.float32)
    for shift_k in range(CONV):
        pre_act = (
            pre_act
            + conv_weight[shift_k] * padded[CONV - 1 - shift_k : CONV - 1 - shift_k + local_tok]
        )
    gate_sig = jax.nn.sigmoid(pre_act)
    unit = (pre_act * gate_sig).reshape(local_tok, SH, P_SIZE)
    bmat = state_input[0].astype(jnp.float32)
    cmat = state_readout[0].astype(jnp.float32)
    rates = log_decay[0]
    cumul = jnp.cumsum(rates, axis=1)
    last_log = cumul[:, -1]
    tail_w = jnp.exp(last_log[:, None] - cumul)
    head_w = jnp.exp(cumul)
    block_decay = jnp.exp(last_log)
    causal = jnp.arange(local_tok)[:, None] >= jnp.arange(local_tok)[None, :]
    decay = jnp.where(
        causal[None],
        jnp.exp(jnp.where(causal[None], cumul[:, :, None] - cumul[:, None, :], 0.0)),
        0.0,
    )
    gram_mat = jnp.dot(state_readout[0], state_input[0].T, preferred_element_type=jnp.float32)
    local_state = jnp.einsum("hs,shp,sn->hpn", tail_w, unit, bmat, precision=top_precision)
    identity = (jnp.ones((SH,), jnp.float32), jnp.zeros((SH, P_SIZE, N), jnp.float32))
    own_block = lax.axis_index("seq")
    block_logs = lax.all_gather(last_log[None], "seq", axis=0, tiled=True)
    prefix = jnp.cumsum(block_logs, axis=0)
    prefix_prev = lax.dynamic_slice_in_dim(prefix, jnp.maximum(own_block - 1, 0), 1, 0)[0]
    pieces = lax.all_gather(
        local_state[None].astype(jnp.bfloat16), "seq", axis=0, tiled=True
    ).astype(jnp.float32)
    piece_rows = pieces.shape[0]
    block_ids = jnp.arange(piece_rows, dtype=jnp.int32)
    earlier_rows = (block_ids < own_block)[:, None]
    weight = jnp.where(
        earlier_rows, jnp.exp(jnp.where(earlier_rows, prefix_prev[None, :] - prefix, 0.0)), 0.0
    )
    entry = jnp.zeros((SH, P_SIZE, N), jnp.float32) + jnp.einsum(
        "jh,jhpn->hpn", weight, pieces, precision=top_precision
    )
    grad_out = ssm_cotangent[0].astype(jnp.float32).reshape(local_tok, SH, P_SIZE)
    local_grad = jnp.einsum("ht,thp,tn->hpn", head_w, grad_out, cmat, precision=top_precision)
    _, leaving = prefix_2((block_decay, local_grad), "seq", chain_combine, identity)
    mixed = gram_mat[None] * decay
    pulled = jnp.einsum("hpn,sn->shp", leaving, bmat, precision=top_precision)
    unit_grad = (
        jnp.einsum("hts,thp->shp", mixed, grad_out, precision=top_precision)
        + jnp.transpose(tail_w)[:, :, None] * pulled
        + skip_gain[None, :, None] * grad_out
    )
    outer = jnp.einsum("thp,shp->hts", grad_out, unit, precision=top_precision)
    gram_grad = jnp.sum(outer * decay, axis=0)
    readout = jnp.einsum("hpn,tn->thp", entry, cmat, precision=top_precision)
    readout_grad = jnp.dot(gram_grad, bmat, precision=top_precision) + jnp.einsum(
        "ht,hpn,thp->tn", head_w, entry, grad_out, precision=top_precision
    )
    b_grad = jnp.dot(gram_grad.T, cmat, precision=top_precision) + jnp.einsum(
        "hs,hpn,shp->sn", tail_w, leaving, unit, precision=top_precision
    )
    direct = outer * mixed
    cumul_grad = jnp.sum(direct, axis=2) - jnp.sum(direct, axis=1)
    cumul_grad = cumul_grad + head_w * jnp.einsum(
        "thp,thp->ht", grad_out, readout, precision=top_precision
    )
    full_end = block_decay[:, None, None] * entry + local_state
    end_term = jnp.sum(leaving * full_end, axis=(1, 2))
    last_slot = (jnp.arange(local_tok) == local_tok - 1).astype(jnp.float32)
    cumul_grad = cumul_grad + end_term[:, None] * last_slot[None, :]
    cumul_grad = cumul_grad - tail_w * jnp.einsum(
        "shp,shp->hs", unit, pulled, precision=top_precision
    )
    decay_grad = jnp.flip(jnp.cumsum(jnp.flip(cumul_grad, axis=1), axis=1), axis=1)
    skip_local = jnp.einsum("thp,thp->h", grad_out, unit, precision=top_precision)
    pre_grad = (
        unit_grad.reshape(local_tok, channels) * gate_sig * (1.0 + pre_act * (1.0 - gate_sig))
    )
    next_rows = passed_along(pre_grad[: CONV - 1], "seq", -1)
    extended = jnp.concatenate([pre_grad, next_rows], axis=0)
    input_grad = jnp.zeros((local_tok, channels), jnp.float32)
    conv_terms = []
    for shift_k in range(CONV):
        input_grad = input_grad + conv_weight[shift_k] * extended[shift_k : shift_k + local_tok]
        conv_terms.append(
            jnp.sum(pre_grad * padded[CONV - 1 - shift_k : CONV - 1 - shift_k + local_tok], axis=0)
        )
    conv_local = jnp.stack(conv_terms, axis=0)
    conv_total, skip_total = lax.psum((conv_local, skip_local), ("dp", "seq"))
    return (
        input_grad.astype(jnp.bfloat16)[None],
        b_grad[None],
        readout_grad[None],
        decay_grad[None],
        skip_total,
        conv_total,
    )


def local(
    query_rows,
    key_rows,
    value_rows,
    out_cotangent,
    turn_lengths,
    ssm_input,
    state_input,
    state_readout,
    log_decay,
    skip_gain,
    conv_weight,
    ssm_cotangent,
):
    attention_out = attention_grads(query_rows, key_rows, value_rows, out_cotangent, turn_lengths)
    ssm_out = ssm_grads(
        ssm_input, state_input, state_readout, log_decay, skip_gain, conv_weight, ssm_cotangent
    )
    return attention_out + ssm_out


def solution(mesh):
    in_specs = (
        P("dp", "seq", None),
        P("dp", "seq", None),
        P("dp", "seq", None),
        P("dp", "seq", None),
        P("dp", None),
        P("dp", "seq", None),
        P("dp", "seq", None),
        P("dp", "seq", None),
        P("dp", None, "seq"),
        P(),
        P(),
        P("dp", "seq", None),
    )
    out_specs = (
        P("dp", "seq", None),
        P("dp", "seq", None),
        P("dp", "seq", None),
        P("dp", "seq", None),
        P("dp", "seq", None),
        P("dp", "seq", None),
        P("dp", None, "seq"),
        P(),
        P(),
    )
    return jax.shard_map(local, mesh=mesh, in_specs=in_specs, out_specs=out_specs, check_vma=False)
```

profile of v0, /device:TPU:0, one launch (start us, length us, event | category | flops | bytes accessed | tf_op | source)
XLA Modules:
  0.0 251.0 jit_solution(3402692336671978117)
XLA Ops:
  7.3 1.3 slice_bitcast_fusion.2
  8.5 2.9 %collective-permute-start = (bf16[3,256]{1,0:T(4,128)(2,1)}, bf16[3,256]{1,0:T(4,128)(2,1)}, u32[]{:S(2)}, u32[]{:S(2)}) collective-permute-start(bf16[3,256]{1,0:T(4,128)(2,1)} %slice_bitcast_fusion.2), channel_id=1, source_target_pairs={{0,1},{1,2},{2,3},{3,4},{4,5},{5,6},{6,7},{7,8},{8,9},{9,10},{10,1... | collective-permute-start | bytes 4616 | tf_op jit(solution)/shard_map/ppermute | solution.py:24
  12.2 1.2 reduce-window.31
  15.6 1.7 fusion.80
  17.5 1.3 broadcast_in_dim.191
  19.7 1.0 copy.133
  20.8 1.0 copy.134
  22.6 24.3 %all-gather = bf16[1,2560,128]{2,1,0:T(8,128)(2,1)S(1)} all-gather(bf16[1,160,128]{2,1,0:T(8,128)(2,1)S(1)} %copy-done.9), channel_id=2, replica_groups=mesh['dp'=2,'seq'=16] {'seq'}, dimensions={1}, use_global_device_ids=true | all-gather | bytes 696320 | tf_op jit(solution)/shard_map/all_gather | solution.py:62
  46.9 20.2 %all-gather.1 = bf16[1,2560,128]{2,1,0:T(8,128)(2,1)S(1)} all-gather(bf16[1,160,128]{2,1,0:T(8,128)(2,1)S(1)} %copy-done.10), channel_id=3, replica_groups=mesh['dp'=2,'seq'=16] {'seq'}, dimensions={1}, use_global_device_ids=true | all-gather | bytes 696320 | tf_op jit(solution)/shard_map/all_gather | solution.py:63
  67.8 27.7 %while.53 = (s32[]{:T(128)}, f32[1,8,160]{2,1,0:T(8,128)S(1)}, f32[1,8,160]{2,1,0:T(8,128)S(1)}, f32[1,8,160,128]{3,2,1,0:T(8,128)S(1)}, s32[1,8]{1,0:T(1,128)},...) while((s32[]{:T(128)}, f32[1,8,160]{2,1,0:T(8,128)S(1)}, ...), condition=%wide.region_7.8_spmd.clone, body=%wide.region_3.7_spmd.clone.sunk | while | flops 1183026816 | bytes 10193015 | solution.py:105
  71.0 2.2 fusion.151
  76.5 2.2 fusion.151
  82.1 2.2 fusion.151
  87.6 2.2 fusion.151
  93.1 2.2 fusion.151
  97.4 34.4 %while.54 = (s32[]{:T(128)}, f32[160,1,8,128]{3,0,2,1:T(8,128)S(1)}, bf16[2560,256]{1,0:T(8,128)(2,1)S(1)}, bf16[2560,128]{1,0:T(8,128)(2,1)S(1)}, s32[1,8]{1,0:...) while((s32[]{:T(128)}, ...), condition=%wide.region_11.12_spmd.clone, body=%wide.region_9.11_spmd.clone.sunk | while | flops 847179904 | bytes 18236584 | solution.py:147
  99.6 1.5 fusion.165
  101.1 2.0 fusion.163
  106.5 1.5 fusion.165
  108.0 2.0 fusion.163
  113.4 1.5 fusion.165
  114.9 2.0 fusion.163
  120.3 1.5 fusion.165
  121.8 2.0 fusion.163
  127.1 1.5 fusion.165
  128.6 2.0 fusion.163
  131.9 1.0 copy-done.1
  133.0 1.2 dynamic-slice
  137.5 32.6 %all-reduce.5 = (f32[64]{0:T(128)S(1)}, f32[64]{0:T(128)S(1)}) all-reduce(f32[64]{0:T(128)S(1)} %bitcast_dynamic-update-slice_fusion, f32[64]{0:T(128)S(1)} %get-tuple-element.835), channel_id=7, replica_groups=mesh['dp'=2,'seq'=16] {'seq'}, use_global_device_ids=true, to_apply=%add.2 | all-reduce | flops 128 | bytes 1024
  171.1 15.8 %while.52 = (s32[]{:T(128)}, f32[4,64,128]{2,1,0:T(8,128)S(1)}, s32[]{:T(128)}, f32[16,4]{1,0:T(8,128)S(1)}, f32[16,4,64,128]{3,2,1,0:T(8,128)}, /*index=5*/s32[]{:T(128)}, s32[]{:T(128)}, s32[]{:T(128)}, s32[]{:T(128)}) while((s32[]{:T(128)}, f32[4,64,128]{2,1,0:T(8,128)S(1)}, s32[]{:T(128)}, f32[16,4]{1,0:T(8,128)S(1)}, ...), condition=%wide.region_16.17_spmd, body=%wide.region_15.16_spmd.sunk | while | flops 65542 | bytes 393419 | solution.py:40
  171.2 1.0 bitcast_add_fusion.4
  172.2 1.0 bitcast_add_fusion.4
  173.2 1.0 bitcast_add_fusion.4
  176.4 1.0 bitcast_add_fusion.4
  177.4 1.0 bitcast_add_fusion.4
  178.4 1.0 bitcast_add_fusion.4
  179.5 1.0 bitcast_add_fusion.4
  180.5 1.0 bitcast_add_fusion.4
  181.5 1.0 bitcast_add_fusion.4
  182.6 1.0 bitcast_add_fusion.4
  183.6 1.0 bitcast_add_fusion.4
  184.7 1.0 bitcast_add_fusion.4
  185.7 1.0 bitcast_add_fusion.4
  190.7 1.4 slice_bitcast_fusion
  192.2 1.3 collective-permute-start.1
  196.0 40.6 %all-reduce.4 = (f32[4]{0:T(128)}, f32[4,256]{1,0:T(4,128)}) all-reduce(f32[4]{0:T(128)S(1)} %multiply_reduce_fusion.1, f32[4,256]{1,0:T(4,128)S(1)} %pad_maximum_fusion.2), channel_id=1, replica_groups=mesh['dp'=2,'seq'=16] {'dp','seq'}, use_global_device_ids=true, to_apply=%region_24.25 | all-reduce | flops 1028 | bytes 8224 | tf_op jit(solution)/shard_map/psum | solution.py:255
  237.3 2.2 fusion.67
  242.0 1.2 reduce-window.33
  (247 shorter events, 56.4 us)
Async XLA Ops:
  7.2 130.1 %copy-start = (bf16[1,160,128]{2,1,0:T(8,128)(2,1)S(1)}, bf16[1,160,128]{2,1,0:T(8,128)(2,1)}, u32[]{:S(2)}) copy-start(bf16[1,160,128]{2,1,0:T(8,128)(2,1)} %param.24) | copy-start | bytes 122884
  7.2 15.4 %copy-start.9 = (bf16[1,160,128]{2,1,0:T(8,128)(2,1)S(1)}, bf16[1,160,128]{2,1,0:T(8,128)(2,1)}, u32[]{:S(2)}) copy-start(bf16[1,160,128]{2,1,0:T(8,128)(2,1)} %param.19) | copy-start | bytes 122884
  7.2 39.7 %copy-start.10 = (bf16[1,160,128]{2,1,0:T(8,128)(2,1)S(1)}, bf16[1,160,128]{2,1,0:T(8,128)(2,1)}, u32[]{:S(2)}) copy-start(bf16[1,160,128]{2,1,0:T(8,128)(2,1)} %param.20) | copy-start | bytes 122884
  7.2 163.9 %all-gather.9.cloned.1.call-start = ((), (), s32[]{:S(2)}) async-start(), calls=%async_computation.2 | async-start | bytes 2228224 | tf_op jit(solution)/shard_map/all_gather | solution.py:31
  8.5 161.6 %collective-permute-start = (bf16[3,256]{1,0:T(4,128)(2,1)}, bf16[3,256]{1,0:T(4,128)(2,1)}, u32[]{:S(2)}, u32[]{:S(2)}) collective-permute-start(bf16[3,256]{1,0:T(4,128)(2,1)} %slice_bitcast_fusion.2), channel_id=1, source_target_pairs={{0,1},{1,2},{2,3},{3,4},{4,5},{5,6},{6,7},{7,8},{8,9},{9,10},{10,1... | collective-permute-start | bytes 4616 | tf_op jit(solution)/shard_map/ppermute | solution.py:24
  13.8 3.7 %copy-start.7 = (f32[1,4,2,128]{3,1,2,0:T(4,128)}, f32[1,4,2,128]{3,1,2,0:T(4,128)S(1)}, u32[]{:S(2)}) copy-start(f32[1,4,2,128]{3,1,2,0:T(4,128)S(1)} %copy.143) | copy-start | bytes 12292
  14.0 3.5 %copy-start.14 = (f32[4,1]{0,1:T(1,128)}, f32[4,1]{0,1:T(1,128)S(1)}, u32[]{:S(2)}) copy-start(f32[4,1]{0,1:T(1,128)S(1)} %copy.116) | copy-start | bytes 52
  14.6 2.9 %copy-start.11 = (f32[160,4]{0,1:T(4,128)}, f32[160,4]{0,1:T(4,128)S(1)}, u32[]{:S(2)}) copy-start(f32[160,4]{0,1:T(4,128)S(1)} %get-tuple-element.832) | copy-start | bytes 7684
  15.6 5.1 %copy-start.2 = (bf16[1,160,256]{1,2,0:T(8,128)(2,1)}, bf16[1,160,256]{1,2,0:T(8,128)(2,1)S(1)}, u32[]{:S(2)}) copy-start(bf16[1,160,256]{1,2,0:T(8,128)(2,1)S(1)} %copy.78) | copy-start | bytes 245764
  17.4 173.3 %reduce-scatter.2.cloned.1.call-start = ((), (), s32[]{:S(2)}) async-start(), calls=%async_computation.1 | async-start | bytes 1392640 | tf_op jit(solution)/shard_map/reduce_scatter | solution.py:150
  95.4 1.2 copy-start.4
  97.4 39.8 %copy-start.5 = (bf16[1,160,128]{2,1,0:T(8,128)(2,1)S(1)}, bf16[1,160,128]{2,1,0:T(8,128)(2,1)}, u32[]{:S(2)}) copy-start(bf16[1,160,128]{2,1,0:T(8,128)(2,1)} %param.25) | copy-start | bytes 122884
  97.4 2.2 copy-start.6
  104.3 2.2 copy-start.6
  111.2 2.2 copy-start.6
  118.1 2.2 copy-start.6
  125.0 2.2 copy-start.6
  131.9 1.1 copy-start.1
  131.9 55.3 %copy-start.3 = (bf16[1,160,256]{1,2,0:T(8,128)(2,1)S(1)}, bf16[1,160,256]{1,2,0:T(8,128)(2,1)}, u32[]{:S(2)}) copy-start(bf16[1,160,256]{1,2,0:T(8,128)(2,1)} %copy-done.2) | copy-start | bytes 245764
  131.9 55.3 %copy-start.13 = (f32[160,4]{0,1:T(4,128)S(1)}, f32[160,4]{0,1:T(4,128)}, u32[]{:S(2)}) copy-start(f32[160,4]{0,1:T(4,128)} %get-tuple-element.831) | copy-start | bytes 7684
  131.9 55.3 %copy-start.16 = (f32[4,160]{1,0:T(4,128)S(1)}, f32[4,160]{1,0:T(4,128)}, u32[]{:S(2)}) copy-start(f32[4,160]{1,0:T(4,128)} %get-tuple-element.833) | copy-start | bytes 7684
  131.9 55.3 %copy-start.17 = (f32[4]{0:T(128)S(1)}, f32[4]{0:T(128)}, u32[]{:S(2)}) copy-start(f32[4]{0:T(128)} %param.27) | copy-start | bytes 52
  132.9 104.4 %all-gather.11.cloned.1.call-start = ((), (), s32[]{:S(2)}) async-start(), calls=%async_computation.3 | async-start | bytes 1114112 | tf_op jit(solution)/shard_map/all_gather | solution.py:197
  192.2 44.4 %collective-permute-start.1 = (f32[3,256]{1,0:T(4,128)S(1)}, f32[3,256]{1,0:T(4,128)S(1)}, u32[]{:S(2)}, u32[]{:S(2)}) collective-permute-start(f32[3,256]{1,0:T(4,128)S(1)} %slice.112), channel_id=1, source_target_pairs={{1,0},{2,1},{3,2},{4,3},{5,4},{6,5},{7,6},{8,7},{9,8},{10,9},{11,1... | collective-permute-start | bytes 9224 | tf_op jit(solution)/shard_map/ppermute | solution.py:24
  193.5 46.1 %copy-start.12 = (f32[160,4]{0,1:T(4,128)S(1)}, f32[160,4]{0,1:T(4,128)}, u32[]{:S(2)}) copy-start(f32[160,4]{0,1:T(4,128)} %copy-done.11) | copy-start | bytes 7684
  194.3 47.3 %copy-start.8 = (f32[1,4,2,128]{3,1,2,0:T(4,128)S(1)}, f32[1,4,2,128]{3,1,2,0:T(4,128)}, u32[]{:S(2)}) copy-start(f32[1,4,2,128]{3,1,2,0:T(4,128)} %copy-done.7) | copy-start | bytes 12292
  194.3 47.3 %copy-start.15 = (f32[4,1]{0,1:T(1,128)S(1)}, f32[4,1]{0,1:T(1,128)}, u32[]{:S(2)}) copy-start(f32[4,1]{0,1:T(1,128)} %copy-done.14) | copy-start | bytes 52
Sparse Core Ops, SparseCore 0:
  17.5 47.2 all-gather.8
  133.1 57.4 reduce-scatter.1
  193.6 36.8 all-gather.10
where the time goes:
time: 253 us; the launch traced here: 251 us
  blocking collectives  118 us (47%)
  matrix products  49.6 us (20%)
  other arithmetic  45.6 us (18%)
  local copies, waits for them, and re-layouts  17.2 us (7%)
  between operations  14.9 us (6%)
  starting transfers between devices  4.34 us (2%)
    psum x1, blocking collectives, ssm_grads(): conv_total, skip_total = lax.psum((conv_local, skip_local), ('dp', 'seq'))  40.6 us
    unnamed x1, blocking collectives  32.6 us
    all_gather x1, blocking collectives, attention_grads(): lax.all_gather(key_rows[0], 'seq', axis=0, tiled=True)  24.3 us
    all_gather x1, blocking collectives, attention_grads(): lax.all_gather(value_rows[0], 'seq', axis=0, tiled=True)  20.2 us
    add x15, other arithmetic, chain_combine(): later[0][:, None, None] * earlier[1] + later[1]  15 us
    dot_general x5, matrix products, first_pass(): jnp.einsum('gqts,sgd->gqtd', expo_terms, value_block.astype(jnp.float32),...  11.2 us
    dot_general x5, matrix products, second_pass(): jnp.einsum('tgqd,sgd->gqts', cotangent, value_block, preferred_element_ty...  9.83 us
    reduce_sum x11, other arithmetic, turn_index(): jnp.sum((positions[:, None] >= bounds[None, :]).astype(jnp.int32), axis=1)  8.25 us
  transfers between devices with their start and end apart: 5, of which 0 were waited for; matrix products, arithmetic and copies ran while one was open for 41% of the time, Pallas kernels for 0%

commit v1 on v0

v1 whole, which is shorter than its diff:
```python
from functools import partial

import jax
import jax.numpy as jnp
from jax import lax
from jax.experimental import pallas as pl
from jax.experimental.pallas import tpu as pltpu
from jax.sharding import PartitionSpec as P

QPG = 8
DH = 128
SH = 4
P_SIZE = 64
N = 128
CONV = 4
CH = SH * P_SIZE
LONGEST_TURN = 1280
NEG_FILL = -1e30
CHUNK = 256
MESH = pl.DeviceIdType.MESH
HI = lax.Precision.HIGHEST
F32 = jnp.float32
BF16 = jnp.bfloat16


def dot_nn(a, b, precision=None):
    return lax.dot_general(
        a, b, (((1,), (0,)), ((), ())), precision=precision, preferred_element_type=F32
    )


def dot_nt(a, b, precision=None):
    return lax.dot_general(
        a, b, (((1,), (1,)), ((), ())), precision=precision, preferred_element_type=F32
    )


def split_nn(a, b):
    top = b.astype(BF16)
    return dot_nn(a, top) + dot_nn(a, (b - top.astype(F32)).astype(BF16))


def kernel(
    count,
    dp_count,
    tok,
    window,
    turn_ref,
    skip_ref,
    q_ref,
    k_ref,
    v_ref,
    do_ref,
    x_ref,
    b_ref,
    c_ref,
    rate_ref,
    conv_ref,
    g_ref,
    dq_ref,
    dk_ref,
    dv_ref,
    dx_ref,
    db_ref,
    dc_ref,
    drate_ref,
    tot_ref,
    qs,
    dos,
    kv,
    prob,
    dprob,
    tops,
    mass,
    delta,
    start_row,
    pos_row,
    pb,
    sb,
    dq_acc,
    dkv_own,
    dkv_out,
    dkv_in,
    rates8,
    rim_out,
    rim_in,
    xpad,
    ext,
    head_out,
    head_in,
    scan_out,
    scan_in,
    unit_s,
    act_s,
    mid_out,
    mid_in,
    sums,
    kv_send,
    kv_recv,
    dkv_send,
    dkv_recv,
    scan_send,
    scan_recv,
    mid_send,
    mid_recv,
    rim_sem,
    head_sem,
    sum_send,
    sum_recv,
):
    me = lax.axis_index("seq")
    my_dp = lax.axis_index("dp")
    rows = QPG * tok
    scale = DH ** (-0.5)

    def remote(src, dst, send, recv, to):
        return pltpu.make_async_remote_copy(
            src_ref=src,
            dst_ref=dst,
            send_sem=send,
            recv_sem=recv,
            device_id=(my_dp, to),
            device_id_type=MESH,
        )

    barrier = pltpu.get_barrier_semaphore()

    @pl.loop(1, count)
    def _(k):
        pl.semaphore_signal(
            barrier, inc=1, device_id=(my_dp, lax.rem(me + k, count)), device_id_type=MESH
        )

    @pl.loop(1, dp_count)
    def _(k):
        pl.semaphore_signal(
            barrier, inc=1, device_id=(lax.rem(my_dp + k, dp_count), me), device_id_type=MESH
        )

    kv[0, :, 0:DH] = k_ref[...]
    kv[0, :, DH:] = v_ref[...]
    rim_out[...] = x_ref[tok - 16 :, :]
    for h in range(QPG):
        qs[h * tok : (h + 1) * tok, :] = q_ref[:, h * DH : (h + 1) * DH]
        dos[h * tok : (h + 1) * tok, :] = do_ref[:, h * DH : (h + 1) * DH]
    lane = lax.broadcasted_iota(jnp.int32, (1, rows), 1)
    place = lane
    for h in range(1, QPG):
        place = jnp.where(lane >= h * tok, lane - h * tok, place)
    place = place + me * tok
    pos_row[...] = place
    begin = jnp.zeros((1, rows), jnp.int32)
    bound = jnp.int32(0)
    for j in range(turn_ref.shape[1]):
        bound = bound + turn_ref[0, j]
        begin = jnp.where(place >= bound, bound, begin)
    start_row[...] = begin
    pl.semaphore_wait(barrier, count - 1 + dp_count - 1)

    rim_copy = remote(rim_out, rim_in, rim_sem.at[0], rim_sem.at[1], lax.rem(me + 1, count))

    @pl.when(me + 1 < count)
    def _():
        rim_copy.start()

    def kv_copy(k, to):
        return remote(kv.at[0], kv.at[k], kv_send.at[k], kv_recv.at[k], to)

    @pl.loop(1, window + 1)
    def _(k):
        @pl.when(me + k < count)
        def _():
            kv_copy(k, lax.rem(me + k, count)).start()

    def gather_pass(k, first):
        keys = kv[k, :, 0:DH]
        values = kv[k, :, DH:]
        key_pos = (me - k) * tok + lax.broadcasted_iota(jnp.int32, (tok, CHUNK), 0)
        for c in range(rows // CHUNK):
            cs = slice(c * CHUNK, (c + 1) * CHUNK)
            s = dot_nt(keys, qs[cs, :]) * scale
            ok = key_pos >= start_row[:, cs]
            if first:
                ok = ok & (key_pos <= pos_row[:, cs])
            s = jnp.where(ok, s, NEG_FILL)
            top = jnp.max(s, axis=0, keepdims=True)
            if not first:
                old = tops[0, :, cs]
                top = jnp.maximum(top, old)
            p = jnp.exp(s - top)
            dp = dot_nt(values, dos[cs, :])
            part = jnp.sum(p, axis=0, keepdims=True)
            part_delta = jnp.sum(p * dp, axis=0, keepdims=True)
            if not first:
                f = jnp.exp(old - top)
                part = part + f * mass[:, cs]
                part_delta = part_delta + f * delta[:, cs]
            mass[:, cs] = part
            delta[:, cs] = part_delta
            tops[0, :, cs] = top
            tops[k + 1, :, cs] = top
            prob[k, :, cs] = p
            dprob[k, :, cs] = dp

    gather_pass(0, True)

    @pl.when(me > 0)
    def _():
        rim_copy.wait_recv()

    @pl.when(me == 0)
    def _():
        rim_in[...] = jnp.zeros_like(rim_in)

    rates8[...] = jnp.zeros_like(rates8)
    rates8[0:SH, :] = rate_ref[...]
    xpad[0:16, :] = rim_in[...].astype(F32)
    xpad[16:, :] = x_ref[...].astype(F32)
    pre = conv_ref[0:1, :] * xpad[16 : 16 + tok, :]
    for t in range(1, CONV):
        pre = pre + conv_ref[t : t + 1, :] * xpad[16 - t : 16 - t + tok, :]
    act_s[...] = pre
    unit_s[...] = pre * jax.nn.sigmoid(pre)

    sub_t = lax.broadcasted_iota(jnp.int32, (tok, tok), 0)
    lane_t = lax.broadcasted_iota(jnp.int32, (tok, tok), 1)
    tri_low = (sub_t >= lane_t).astype(F32)
    tri_up = (sub_t <= lane_t).astype(F32)
    head_of = lax.broadcasted_iota(jnp.int32, (8, CH), 1)
    head_id = lax.broadcasted_iota(jnp.int32, (8, CH), 0)
    picks = ((head_of >= head_id * P_SIZE) & (head_of < (head_id + 1) * P_SIZE)).astype(F32)
    cum_col = dot_nt(tri_low, rates8[...], HI)
    cum_row = dot_nn(rates8[...], tri_up, HI)
    cum_wide = dot_nn(cum_col, picks, HI)
    last_wide = cum_wide[tok - 1 : tok, :]
    tail_wide = jnp.exp(last_wide - cum_wide)
    head_wide = jnp.exp(cum_wide)
    gout = g_ref[...]
    b_turned = b_ref[...].astype(F32).T.astype(BF16)
    c_turned = c_ref[...].astype(F32).T.astype(BF16)
    tail_unit = tail_wide * unit_s[...]
    head_gout = head_wide * gout.astype(F32)

    def log_rows(a):
        return jnp.broadcast_to(a, (8, CH))

    for way, (turned, right) in enumerate(((b_turned, tail_unit), (c_turned, head_gout))):
        scan_out[way, 0:N, :] = split_nn(turned, right)
        scan_out[way, N:, :] = log_rows(last_wide)

    def toward(way, k):
        return me + k if way == 0 else me - k

    def inside(i):
        return (i >= 0) & (i < count)

    def scan_copy(way, k):
        return remote(
            scan_out.at[way],
            scan_in.at[way, k - 1],
            scan_send.at[way, k - 1],
            scan_recv.at[way, k - 1],
            lax.rem(toward(way, k) + count, count),
        )

    def mid_copy(way, k):
        return remote(
            mid_out.at[way],
            mid_in.at[way, k - 1],
            mid_send.at[way, k - 1],
            mid_recv.at[way, k - 1],
            lax.rem(toward(way, 4 * k) + count, count),
        )

    mids = -(-count // 4) - 1

    def send_all(make, step, steps):
        for way in range(2):
            for k in range(1, steps + 1):

                @pl.when(inside(toward(way, step * k)))
                def _():
                    make(way, k).start()

    def receive_all(make, into, step, steps):
        for way in range(2):
            for k in range(1, steps + 1):
                here = inside(toward(1 - way, step * k))

                @pl.when(here)
                def _():
                    make(way, k).wait_recv()

                @pl.when(jnp.logical_not(here))
                def _():
                    into[way, k - 1] = jnp.zeros(into.shape[2:], F32)

    def log_of(ref, way, k):
        return ref[way, k - 1, N : N + 1, :]

    send_all(scan_copy, 1, 4)

    def later_blocks(low, high):
        @pl.loop(low, high)
        def _(k):
            @pl.when(me >= k)
            def _():
                kv_copy(k, lax.rem(me + k, count)).wait_recv()
                gather_pass(k, False)

    half = window // 2
    later_blocks(1, half + 1)

    receive_all(scan_copy, scan_in, 1, 4)
    near = []
    for way in range(2):
        total = jnp.zeros((N, CH), F32)
        logs = jnp.zeros((1, CH), F32)
        for k in range(1, 5):
            total = total + jnp.exp(logs) * scan_in[way, k - 1, 0:N, :]
            logs = logs + log_of(scan_in, way, k)
        mid_out[way, 0:N, :] = total
        mid_out[way, N:, :] = log_rows(logs)
        near.append(logs)
    send_all(mid_copy, 4, mids)

    later_blocks(half + 1, window + 1)

    dq_acc[...] = jnp.zeros_like(dq_acc)

    def grad_pass(k):
        for c in range(rows // CHUNK):
            cs = slice(c * CHUNK, (c + 1) * CHUNK)
            inv = 1.0 / mass[:, cs]
            f = jnp.exp(tops[k + 1, :, cs] - tops[0, :, cs]) * inv
            p = prob[k, :, cs] * f
            s = (p * scale) * (dprob[k, :, cs] - delta[:, cs] * inv)
            pb[:, cs] = p.astype(BF16)
            sb[:, cs] = s.astype(BF16)
        keys_turned = kv[k, :, 0:DH].astype(F32).T.astype(BF16)
        dq_acc[...] += dot_nn(keys_turned, sb[...])
        return dot_nn(sb[...], qs[...]), dot_nn(pb[...], dos[...])

    def dkv_copy(k, to):
        return remote(dkv_out.at[k - 1], dkv_in.at[k - 1], dkv_send.at[k], dkv_recv.at[k], to)

    @pl.loop(0, window)
    def _(i):
        k = window - i

        @pl.when(me >= k)
        def _():
            dk, dv = grad_pass(k)
            dkv_out[k - 1, :, 0:DH] = dk.astype(BF16)
            dkv_out[k - 1, :, DH:] = dv.astype(BF16)
            dkv_copy(k, lax.rem(me - k + count, count)).start()

    own_dk, own_dv = grad_pass(0)
    dkv_own[:, 0:DH] = own_dk
    dkv_own[:, DH:] = own_dv
    dq_turned = dq_acc[...].T
    for h in range(QPG):
        dq_ref[:, h * DH : (h + 1) * DH] = dq_turned[h * tok : (h + 1) * tok, :].astype(BF16)

    receive_all(mid_copy, mid_in, 4, mids)
    states = []
    for way in range(2):
        total = mid_out[way, 0:N, :]
        logs = near[way]
        for k in range(1, mids + 1):
            total = total + jnp.exp(logs) * mid_in[way, k - 1, 0:N, :]
            logs = logs + log_of(mid_in, way, k)
        states.append(total)
    entry, leaving = states
    entry_b, leaving_b = entry.astype(BF16), leaving.astype(BF16)

    bmat, cmat = b_ref[...], c_ref[...]
    unit = unit_s[...]
    gout_wide = gout.astype(F32)
    pulled = tail_wide * split_nn(bmat, leaving)
    readout = head_wide * split_nn(cmat, entry)
    gram = dot_nt(bmat, cmat)
    lane_c = lax.broadcasted_iota(jnp.int32, (1, CH), 1)
    skip_wide = jnp.zeros((1, CH), F32)
    unit_grad = pulled
    gram_grad = jnp.zeros((tok, tok), F32)
    ones8 = jnp.ones((8, tok), F32)
    row8 = lax.broadcasted_iota(jnp.int32, (8, tok), 0)
    flow = jnp.zeros((8, tok), F32)
    for h in range(SH):
        mine = (lane_c >= h * P_SIZE) & (lane_c < (h + 1) * P_SIZE)
        skip_wide = jnp.where(mine, skip_ref[h], skip_wide)
        gap = jnp.minimum(cum_row[h : h + 1, :] - cum_col[:, h : h + 1], 0.0)
        decay = jnp.where(lane_t >= sub_t, jnp.exp(gap), 0.0)
        mixed = gram * decay
        unit_h = jnp.where(mine, unit, 0.0)
        unit_top = unit_h.astype(BF16)
        unit_rest = (unit_h - unit_top.astype(F32)).astype(BF16)
        gout_h = jnp.where(mine, gout_wide, 0.0).astype(BF16)
        unit_grad = unit_grad + dot_nn(mixed.astype(BF16), gout_h)
        outer = dot_nt(unit_top, gout) + dot_nt(unit_rest, gout)
        gram_grad = gram_grad + outer * decay
        direct = outer * mixed
        flow_h = jnp.sum(direct, axis=0, keepdims=True) - dot_nt(ones8, direct, HI)
        flow = jnp.where(row8 == h, flow_h, flow)
    unit_grad = unit_grad + skip_wide * gout_wide
    pre = act_s[...]
    sig = jax.nn.sigmoid(pre)
    pre_grad = unit_grad * sig * (1.0 + pre * (1.0 - sig))
    ext[0:tok, :] = pre_grad
    head_out[...] = ext[0:8, :]
    head_copy = remote(
        head_out, head_in, head_sem.at[0], head_sem.at[1], lax.rem(me + count - 1, count)
    )

    @pl.when(me > 0)
    def _():
        head_copy.start()

    sum_row = lax.broadcasted_iota(jnp.int32, (8, CH), 0)
    local = jnp.zeros((8, CH), F32)
    for t in range(CONV):
        term = jnp.sum(pre_grad * xpad[16 - t : 16 - t + tok, :], axis=0, keepdims=True)
        local = jnp.where(sum_row == t, term, local)
    local = jnp.where(sum_row == CONV, jnp.sum(gout_wide * unit, axis=0, keepdims=True), local)

    line, column = me // 4, me % 4
    groups = (
        (count // 4, line, lambda j: (my_dp, j * 4 + column)),
        (4, column, lambda j: (my_dp, line * 4 + j)),
        (dp_count, my_dp, lambda j: (j, me)),
    )

    def sum_copy(g, own, j, to, slot):
        return pltpu.make_async_remote_copy(
            src_ref=sums.at[g, own],
            dst_ref=sums.at[g, slot],
            send_sem=sum_send.at[g, j],
            recv_sem=sum_recv.at[g, slot],
            device_id=to,
            device_id_type=MESH,
        )

    def sum_start(g, value):
        size, own, where = groups[g]
        sums[g, own] = value
        for j in range(size):

            @pl.when(own != j)
            def _():
                sum_copy(g, own, j, where(j), own).start()

    def sum_finish(g):
        size, own, where = groups[g]
        for j in range(size):

            @pl.when(own != j)
            def _():
                copy = sum_copy(g, own, j, where(j), j)
                copy.wait_send()
                copy.wait_recv()

        value = sums[g, 0]
        for j in range(1, size):
            value = value + sums[g, j]
        return value

    sum_start(0, local)
    gram_grad_b = gram_grad.astype(BF16)
    db_ref[...] = dot_nn(gram_grad_b, cmat) + dot_nt(tail_unit.astype(BF16), leaving_b)
    gram_turned = gram_grad.T.astype(BF16)
    dc_ref[...] = dot_nn(gram_turned, bmat) + dot_nt(head_gout.astype(BF16), entry_b)
    sum_start(1, sum_finish(0))
    flow = flow + dot_nt(picks, gout_wide * readout, HI)
    kept = dot_nt(picks, unit * pulled, HI)
    ends = jnp.exp(last_wide) * jnp.sum(leaving * entry, axis=0, keepdims=True)
    end = dot_nt(picks, jnp.broadcast_to(ends, (8, CH)), HI)
    strict_up = (sub_t < lane_t).astype(F32)
    drate = dot_nn(flow, tri_low, HI) + dot_nn(kept, strict_up, HI) + end[:, 0:1]
    drate_ref[...] = drate[0:SH, :]
    sum_start(2, sum_finish(1))

    @pl.when(me + 1 < count)
    def _():
        head_copy.wait_recv()

    @pl.when(me + 1 == count)
    def _():
        head_in[...] = jnp.zeros_like(head_in)

    ext[tok:, :] = head_in[...]
    dx = conv_ref[0:1, :] * ext[0:tok, :]
    for t in range(1, CONV):
        dx = dx + conv_ref[t : t + 1, :] * ext[t : t + tok, :]
    dx_ref[...] = dx.astype(BF16)
    tot_ref[...] = sum_finish(2)

    @pl.loop(1, window + 1)
    def _(k):
        @pl.when(me + k < count)
        def _():
            dkv_copy(k, lax.rem(me + k, count)).wait_recv()
            dkv_own[...] += dkv_in[k - 1].astype(F32)
            kv_copy(k, lax.rem(me + k, count)).wait_send()

        @pl.when(me >= k)
        def _():
            dkv_copy(k, lax.rem(me - k + count, count)).wait_send()

    dk_ref[...] = dkv_own[:, 0:DH].astype(BF16)
    dv_ref[...] = dkv_own[:, DH:].astype(BF16)

    @pl.when(me + 1 < count)
    def _():
        rim_copy.wait_send()

    @pl.when(me > 0)
    def _():
        head_copy.wait_send()

    for make, step, steps in ((scan_copy, 1, 4), (mid_copy, 4, mids)):
        for way in range(2):
            for k in range(1, steps + 1):

                @pl.when(inside(toward(way, step * k)))
                def _():
                    make(way, k).wait_send()


def local(
    count,
    dp_count,
    query_rows,
    key_rows,
    value_rows,
    out_cotangent,
    turn_lengths,
    ssm_input,
    state_input,
    state_readout,
    log_decay,
    skip_gain,
    conv_weight,
    ssm_cotangent,
):
    tok = query_rows.shape[1]
    rows = QPG * tok
    window = min(count - 1, -(-(LONGEST_TURN - 1) // tok))
    slots = window + 1
    mids = -(-count // 4) - 1
    span = max(count // 4, 4, dp_count)
    vmem = pl.BlockSpec(memory_space=pltpu.VMEM)
    smem = pl.BlockSpec(memory_space=pltpu.SMEM)
    dma = pltpu.SemaphoreType.DMA
    outs = pl.pallas_call(
        partial(kernel, count, dp_count, tok, window),
        out_shape=(
            jax.ShapeDtypeStruct((tok, QPG * DH), BF16),
            jax.ShapeDtypeStruct((tok, DH), BF16),
            jax.ShapeDtypeStruct((tok, DH), BF16),
            jax.ShapeDtypeStruct((tok, CH), BF16),
            jax.ShapeDtypeStruct((tok, N), F32),
            jax.ShapeDtypeStruct((tok, N), F32),
            jax.ShapeDtypeStruct((SH, tok), F32),
            jax.ShapeDtypeStruct((8, CH), F32),
        ),
        in_specs=[smem, smem] + [vmem] * 10,
        out_specs=(vmem,) * 8,
        scratch_shapes=[
            pltpu.VMEM((rows, DH), BF16),
            pltpu.VMEM((rows, DH), BF16),
            pltpu.VMEM((slots, tok, 2 * DH), BF16),
            pltpu.VMEM((slots, tok, rows), F32),
            pltpu.VMEM((slots, tok, rows), F32),
            pltpu.VMEM((slots + 1, 1, rows), F32),
            pltpu.VMEM((1, rows), F32),
            pltpu.VMEM((1, rows), F32),
            pltpu.VMEM((1, rows), jnp.int32),
            pltpu.VMEM((1, rows), jnp.int32),
            pltpu.VMEM((tok, rows), BF16),
            pltpu.VMEM((tok, rows), BF16),
            pltpu.VMEM((DH, rows), F32),
            pltpu.VMEM((tok, 2 * DH), F32),
            pltpu.VMEM((window, tok, 2 * DH), BF16),
            pltpu.VMEM((window, tok, 2 * DH), BF16),
            pltpu.VMEM((8, tok), F32),
            pltpu.VMEM((16, CH), BF16),
            pltpu.VMEM((16, CH), BF16),
            pltpu.VMEM((16 + tok, CH), F32),
            pltpu.VMEM((tok + 8, CH), F32),
            pltpu.VMEM((8, CH), F32),
            pltpu.VMEM((8, CH), F32),
            pltpu.VMEM((2, N + 8, CH), F32),
            pltpu.VMEM((2, 4, N + 8, CH), F32),
            pltpu.VMEM((tok, CH), F32),
            pltpu.VMEM((tok, CH), F32),
            pltpu.VMEM((2, N + 8, CH), F32),
            pltpu.VMEM((2, mids, N + 8, CH), F32),
            pltpu.VMEM((3, span, 8, CH), F32),
            dma((slots,)),
            dma((slots,)),
            dma((slots,)),
            dma((slots,)),
            dma((2, 4)),
            dma((2, 4)),
            dma((2, mids)),
            dma((2, mids)),
            dma((2,)),
            dma((2,)),
            dma((3, span)),
            dma((3, span)),
        ],
        compiler_params=pltpu.CompilerParams(
            collective_id=0, has_side_effects=True, vmem_limit_bytes=48 * 1024 * 1024
        ),
    )(
        turn_lengths,
        skip_gain,
        query_rows[0],
        key_rows[0],
        value_rows[0],
        out_cotangent[0],
        ssm_input[0],
        state_input[0],
        state_readout[0],
        log_decay[0],
        conv_weight,
        ssm_cotangent[0],
    )
    dq, dk, dv, dx, db, dc, drate, totals = outs
    skip = jnp.sum(totals[CONV].reshape(SH, P_SIZE), axis=1)
    return (dq[None], dk[None], dv[None], dx[None], db[None], dc[None], drate[None], skip, totals[:CONV])


def solution(mesh):
    row = P("dp", "seq", None)
    in_specs = (row, row, row, row, P("dp", None), row, row, row, P("dp", None, "seq"), P(), P(), row)
    out_specs = (row, row, row, row, row, row, P("dp", None, "seq"), P(), P())
    return jax.shard_map(
        partial(local, mesh.shape["seq"], mesh.shape["dp"]),
        mesh=mesh,
        in_specs=in_specs,
        out_specs=out_specs,
        check_vma=False,
    )
```

time: 253 us -> 83.1 us (0.33)
  blocking collectives: 118 us -> 0 us
  Pallas kernels: 0 us -> 68.6 us
  matrix products: 49.6 us -> 0 us
  other arithmetic: 45.6 us -> 0.63 us
  between operations: 14.9 us -> 0.7 us
  local copies, waits for them, and re-layouts: 17.2 us -> 12.7 us
  starting transfers between devices: 4.34 us -> 0 us
    pallas_call x0 -> x1, Pallas kernels: none -> 68.6 us  [local(): pl.pallas_call(partial(kernel, count, dp_count, tok, window), out_shape=(...]
    dot_general x47 -> x0, matrix products: 49.6 us -> none  [the longest x5 11.2 us: first_pass(): jnp.einsum('gqts,sgd->gqtd', expo_terms, value_block.astype(jnp.float32),...]
    all_gather x2 -> x0, blocking collectives: 44.5 us -> none  [the longest x1 24.3 us: attention_grads(): lax.all_gather(key_rows[0], 'seq', axis=0, tiled=True)]
    psum x1 -> x0, blocking collectives: 40.6 us -> none  [ssm_grads(): conv_total, skip_total = lax.psum((conv_local, skip_local), ('dp', 'seq'))]
    unnamed x1 -> x0, blocking collectives: 32.6 us -> none
    add x42 -> x0, other arithmetic: 15.7 us -> none  [the longest x15 15 us: chain_combine(): later[0][:, None, None] * earlier[1] + later[1]]
    reduce_sum x19 -> x1, other arithmetic: 14 us -> 0.63 us  [local(): skip = jnp.sum(totals[CONV].reshape(SH, P_SIZE), axis=1)]
    and x10 -> x0, other arithmetic: 8.1 us -> none  [block_keys(): (key_pos[None, :] <= own_pos[:, None]) & (turn_index(lengths, key_pos)[No...]
  transfers between devices with their start and end apart: 5 -> 0, of which waited for: 0 -> 0; matrix products, arithmetic and copies ran while one was open for 41% -> 0% of each run, Pallas kernels for 0% -> 0%
where the time goes in v1:
time: 83.1 us; the launch traced here: 82.5 us
  Pallas kernels  68.6 us (83%)
  local copies, waits for them, and re-layouts  12.7 us (15%)
    pallas_call x1, Pallas kernels, local(): pl.pallas_call(partial(kernel, count, dp_count, tok, window), out_shape=(...  68.6 us
    unnamed x31, local copies, waits for them, and re-layouts  12 us

profile of v1, /device:TPU:0, one launch (start us, length us, event | category | flops | bytes accessed | tf_op | source)
XLA Modules:
  0.0 82.5 jit_solution(99182594100169870)
XLA Ops:
  0.6 0.0 copy-start.9
  0.7 0.0 copy-start.8
  0.7 0.0 copy-start.10
  0.7 0.0 copy-start.11
  0.7 0.6 copy-done.9
  1.3 0.0 copy-done.8
  1.4 0.0 copy-done.10
  1.4 0.0 copy-done.11
  1.4 0.0 copy-start
  1.4 1.0 %copy-done = bf16[1,160,1024]{2,1,0:T(8,128)(2,1)S(1)} copy-done((bf16[1,160,1024]{2,1,0:T(8,128)(2,1)S(1)}, bf16[1,160,1024]{2,1,0:T(8,128)(2,1)}, u32[]{:S(2)}) %copy-start) | copy-done | bytes 327704
  2.3 0.0 copy-start.1
  2.3 1.0 %copy-done.1 = bf16[1,160,1024]{2,1,0:T(8,128)(2,1)S(1)} copy-done((bf16[1,160,1024]{2,1,0:T(8,128)(2,1)S(1)}, bf16[1,160,1024]{2,1,0:T(8,128)(2,1)}, u32[]{:S(2)}) %copy-start.1) | copy-done | bytes 327704
  3.3 0.0 copy-start.2
  3.3 0.9 %copy-done.2 = bf16[1,160,256]{2,1,0:T(8,128)(2,1)S(1)} copy-done((bf16[1,160,256]{2,1,0:T(8,128)(2,1)S(1)}, bf16[1,160,256]{2,1,0:T(8,128)(2,1)}, u32[]{:S(2)}) %copy-start.2) | copy-done | bytes 81944
  4.2 0.0 copy-start.3
  4.2 0.9 %copy-done.3 = bf16[1,160,256]{2,1,0:T(8,128)(2,1)S(1)} copy-done((bf16[1,160,256]{2,1,0:T(8,128)(2,1)S(1)}, bf16[1,160,256]{2,1,0:T(8,128)(2,1)}, u32[]{:S(2)}) %copy-start.3) | copy-done | bytes 81944
  5.1 0.0 copy-start.4
  5.1 0.8 copy-done.4
  5.9 0.0 copy-start.5
  5.9 0.8 copy-done.5
  6.6 0.0 copy-start.6
  6.6 0.8 copy-done.6
  7.4 0.0 copy-start.7
  7.4 0.8 copy-done.7
  8.2 68.6 %shard_map.187 = (bf16[160,1024]{1,0:T(8,128)(2,1)S(1)}, bf16[160,128]{1,0:T(8,128)(2,1)S(1)}, bf16[160,128]{1,0:T(8,128)(2,1)S(1)}, bf16[160,256]{1,0:T(8,128)(...) custom-call(s32[1,8]{1,0:T(1,128)S(1)} %copy-done.10, ...), custom_call_target="tpu_custom_call" | custom-call | tf_op jit(solution)/shard_map/pallas_call | solution.py:555
  76.8 0.6 slice.7
  77.4 0.1 reshape_squeeze.3
  77.5 0.6 reduce_sum.9
  78.1 0.7 copy.28
  78.8 0.6 copy.29
  79.4 0.6 copy.30
  80.0 0.6 copy.31
  80.7 0.6 copy.32
  81.3 0.6 copy.33
  82.0 0.6 copy.34
  (1 shorter events, 0.0 us)
Async XLA Ops:
  0.6 0.7 copy-start.9
  0.7 0.7 copy-start.8
  0.7 0.7 copy-start.10
  0.7 0.7 copy-start.11
  1.4 1.0 %copy-start = (bf16[1,160,1024]{2,1,0:T(8,128)(2,1)S(1)}, bf16[1,160,1024]{2,1,0:T(8,128)(2,1)}, u32[]{:S(2)}) copy-start(bf16[1,160,1024]{2,1,0:T(8,128)(2,1)} %param.12) | copy-start | bytes 983044
  2.3 1.0 %copy-start.1 = (bf16[1,160,1024]{2,1,0:T(8,128)(2,1)S(1)}, bf16[1,160,1024]{2,1,0:T(8,128)(2,1)}, u32[]{:S(2)}) copy-start(bf16[1,160,1024]{2,1,0:T(8,128)(2,1)} %param.15) | copy-start | bytes 983044
  3.3 0.9 %copy-start.2 = (bf16[1,160,256]{2,1,0:T(8,128)(2,1)S(1)}, bf16[1,160,256]{2,1,0:T(8,128)(2,1)}, u32[]{:S(2)}) copy-start(bf16[1,160,256]{2,1,0:T(8,128)(2,1)} %param.17) | copy-start | bytes 245764
  4.2 0.9 %copy-start.3 = (bf16[1,160,256]{2,1,0:T(8,128)(2,1)S(1)}, bf16[1,160,256]{2,1,0:T(8,128)(2,1)}, u32[]{:S(2)}) copy-start(bf16[1,160,256]{2,1,0:T(8,128)(2,1)} %param.23) | copy-start | bytes 245764
  5.1 0.8 copy-start.4
  5.9 0.8 copy-start.5
  6.6 0.8 copy-start.6
  7.4 0.8 copy-start.7
